TPU v7x, 32 devices: a whole 2x2x4 slice. The times are simulated.
32 devices in a mesh: dp: 16 (over z, y, x), tensor: 2 (over core).
Axes of the slice: x: 2, y: 2, z: 4, core: 2. Of those that a mesh axis runs over, the one named last changes fastest.
Arguments:
- tokens: bfloat16 [16384, 768], P(('dp', 'tensor')), may hold values from -6 to 6
- lengths: int32 [16], P('dp'), may hold values from 1 to 1024, 10240 in all
- qkv_weight: bfloat16 [3, 768, 768], P(None, 'dp', 'tensor'), may hold values from -0.21875 to 0.21875
- qv_bias: float32 [2, 768], P(None, 'tensor'), may hold values from -3 to 3
- out_weight: bfloat16 [768, 768], P('tensor', 'dp'), may hold values from -0.875 to 0.875
- out_bias: float32 [768], replicated, may hold values from -3 to 3
- up_weight: bfloat16 [768, 3072], P('dp', 'tensor'), may hold values from -0.21875 to 0.21875
- up_bias: float32 [3072], P('tensor'), may hold values from -3 to 3
- down_weight: bfloat16 [3072, 768], P('tensor', 'dp'), may hold values from -0.109375 to 0.109375
- down_bias: float32 [768], replicated, may hold values from -3 to 3
- norm1_gain: float32 [768], replicated, may hold values from 0.5 to 1.5
- norm1_shift: float32 [768], replicated, may hold values from -3 to 3
- norm2_gain: float32 [768], replicated, may hold values from 0.5 to 1.5
- norm2_shift: float32 [768], replicated, may hold values from -3 to 3
- cotangent: bfloat16 [16384, 768], P(('dp', 'tensor')), may hold values from -6 to 6
Outputs:
- layer_output: bfloat16 [16384, 768], P(('dp', 'tensor'))
- input_grad: bfloat16 [16384, 768], P(('dp', 'tensor'))
- grad_qkv_weight: float32 [3, 768, 768], P(None, 'dp', 'tensor')
- grad_qv_bias: float32 [2, 768], P(None, 'tensor')
- grad_out_weight: float32 [768, 768], P('tensor', 'dp')
- grad_out_bias: float32 [768], replicated
- grad_up_weight: float32 [768, 3072], P('dp', 'tensor')
- grad_up_bias: float32 [3072], P('tensor')
- grad_down_weight: float32 [3072, 768], P('tensor', 'dp')
- grad_down_bias: float32 [768], replicated
- grad_norm1_gain: float32 [768], replicated
- grad_norm1_shift: float32 [768], replicated
- grad_norm2_gain: float32 [768], replicated
- grad_norm2_shift: float32 [768], replicated
Inputs may be any that keep to these rules, and one draw needn't show every extreme that they name: lengths[s] is the count of real tokens of sequence s; some sequence has 1024.
All inputs are finite; a program needn't handle non-finite values. No bound on the sum of `lengths` on one device may be relied on, other than what follows from the above.
Results may differ from a plain program's by a relative error of at most 0.017.
Values may be sent and summed in bfloat16 or wider, within the bound.
A program may use at most 192 MiB of HBM per device.

v0:
```python
import jax
import jax.numpy as jnp
from jax import lax
from jax.sharding import PartitionSpec as P

HEAD_DIM = 64
LENGTH = 1024
EPSILON = 1e-05
NEGATIVE = -1e30


def layer_norm(values, norm_gain, norm_shift):
    center = values - jnp.mean(values, axis=-1, keepdims=True)
    spread = jnp.mean(center * center, axis=-1, keepdims=True)
    return center * lax.rsqrt(spread + EPSILON) * norm_gain + norm_shift


def gelu_exact(values):
    return jax.nn.gelu(values, approximate=False)


def matmul(left, right):
    return jnp.dot(left, right, preferred_element_type=jnp.float32)


def contract_rows(left, right):
    return lax.dot_general(
        left, right, (((0,), (0,)), ((), ())), preferred_element_type=jnp.float32
    )


def contract_cols(left, right):
    return lax.dot_general(
        left, right, (((1,), (1,)), ((), ())), preferred_element_type=jnp.float32
    )


def per_device(
    tokens,
    lengths,
    qkv_weight,
    qv_bias,
    out_weight,
    out_bias,
    up_weight,
    up_bias,
    down_weight,
    down_bias,
    norm1_gain,
    norm1_shift,
    norm2_gain,
    norm2_shift,
    cotangent,
):
    tok_rows = tokens.shape[0]
    local_width = qkv_weight.shape[2]
    head_count = local_width // HEAD_DIM
    seq_count = lengths.shape[0]
    block_rows = min(512, LENGTH)
    scaling = HEAD_DIM ** (-0.5)
    positions = jnp.arange(LENGTH)
    qkv_full, out_full, up_full, down_full = (
        lax.all_gather(qkv_weight, "dp", axis=1, tiled=True),
        lax.all_gather(out_weight, "dp", axis=1, tiled=True),
        lax.all_gather(up_weight, "dp", axis=0, tiled=True),
        lax.all_gather(down_weight, "dp", axis=1, tiled=True),
    )
    gathered = lax.all_gather(tokens, "tensor", axis=0, tiled=True)
    queries = (matmul(gathered, qkv_full[0]) + qv_bias[0]).astype(jnp.bfloat16)
    key_rows = matmul(gathered, qkv_full[1]).astype(jnp.bfloat16)
    value_rows = (matmul(gathered, qkv_full[2]) + qv_bias[1]).astype(jnp.bfloat16)

    def forward_seq(packed):
        seq_queries, seq_keys, seq_values, length = packed
        query_heads = seq_queries.reshape(LENGTH, head_count, HEAD_DIM)
        key_heads = seq_keys.reshape(LENGTH, head_count, HEAD_DIM)
        value_heads = seq_values.reshape(LENGTH, head_count, HEAD_DIM)
        usable = (positions < length)[None, None, :]
        context_blocks = []
        total_blocks = []
        for block_start in range(0, LENGTH, block_rows):
            block_q = query_heads[block_start : block_start + block_rows]
            scores = (
                jnp.einsum("qhd,khd->hqk", block_q, key_heads, preferred_element_type=jnp.float32)
                * scaling
            )
            scores = jnp.where(usable, scores, NEGATIVE)
            row_top = jnp.max(scores, axis=-1, keepdims=True)
            exponent = jnp.exp(scores - row_top)
            row_total = jnp.sum(exponent, axis=-1, keepdims=True)
            weights = (exponent / row_total).astype(jnp.bfloat16)
            block_context = jnp.einsum(
                "hqk,khd->qhd", weights, value_heads, preferred_element_type=jnp.float32
            )
            context_blocks.append(block_context.reshape(block_rows, local_width))
            total_blocks.append((row_top + jnp.log(row_total))[..., 0])
        return (
            jnp.concatenate(context_blocks, axis=0).astype(jnp.bfloat16),
            jnp.concatenate(total_blocks, axis=1),
        )

    shaped = (
        queries.reshape(seq_count, LENGTH, local_width),
        key_rows.reshape(seq_count, LENGTH, local_width),
        value_rows.reshape(seq_count, LENGTH, local_width),
    )
    contexts, log_totals = lax.map(forward_seq, (shaped[0], shaped[1], shaped[2], lengths))
    context_flat = contexts.reshape(seq_count * LENGTH, local_width)
    row_block = lax.slice_in_dim(context_flat, 0, tok_rows * lax.axis_size("tensor"), axis=0)
    attn = (
        lax.psum_scatter(matmul(row_block, out_full), "tensor", scatter_dimension=0, tiled=True)
        + out_bias
    )
    first_sum = tokens.astype(jnp.float32) + attn
    hidden = layer_norm(first_sum, norm1_gain, norm1_shift)
    hidden_low = hidden.astype(jnp.bfloat16)
    hidden_all = lax.all_gather(hidden_low, "tensor", axis=0, tiled=True)
    upper = matmul(hidden_all, up_full) + up_bias
    active = gelu_exact(upper).astype(jnp.bfloat16)
    row_block = lax.slice_in_dim(active, 0, tok_rows * lax.axis_size("tensor"), axis=0)
    ffn_out = (
        lax.psum_scatter(matmul(row_block, down_full), "tensor", scatter_dimension=0, tiled=True)
        + down_bias
    )
    second_sum = hidden + ffn_out
    layer_output = layer_norm(second_sum, norm2_gain, norm2_shift).astype(jnp.bfloat16)
    qkv_back, out_back, up_back, down_back = (qkv_full, out_full, up_full, down_full)
    unused_two, norm_two_back = jax.vjp(layer_norm, second_sum, norm2_gain, norm2_shift)
    grad_second, gain_two_grad, shift_two_grad = norm_two_back(cotangent.astype(jnp.float32))
    grad_ffn = grad_second.astype(jnp.bfloat16)
    down_bias_grad = jnp.sum(grad_ffn.astype(jnp.float32), axis=0)
    grad_ffn_all = lax.all_gather(grad_ffn, "tensor", axis=0, tiled=True)
    down_weight_grad = contract_rows(active, grad_ffn_all)
    grad_active = contract_cols(grad_ffn_all, down_back)
    unused_gelu, gelu_back = jax.vjp(gelu_exact, upper)
    grad_upper = gelu_back(grad_active)[0].astype(jnp.bfloat16)
    up_bias_grad = jnp.sum(grad_upper.astype(jnp.float32), axis=0)
    up_weight_grad = contract_rows(hidden_all, grad_upper)
    row_block = lax.slice_in_dim(grad_upper, 0, tok_rows * lax.axis_size("tensor"), axis=0)
    grad_hidden = grad_second + lax.psum_scatter(
        contract_cols(row_block, up_back), "tensor", scatter_dimension=0, tiled=True
    )
    unused_one, norm_one_back = jax.vjp(layer_norm, first_sum, norm1_gain, norm1_shift)
    grad_first, gain_one_grad, shift_one_grad = norm_one_back(grad_hidden)
    grad_attn = grad_first.astype(jnp.bfloat16)
    out_bias_grad = jnp.sum(grad_attn.astype(jnp.float32), axis=0)
    grad_attn_all = lax.all_gather(grad_attn, "tensor", axis=0, tiled=True)
    out_weight_grad = contract_rows(context_flat, grad_attn_all)
    grad_context = contract_cols(grad_attn_all, out_back).astype(jnp.bfloat16)

    def backward_seq(packed):
        seq_queries, seq_keys, seq_values, length, seq_grad, seq_totals = packed
        query_heads = seq_queries.reshape(LENGTH, head_count, HEAD_DIM)
        key_heads = seq_keys.reshape(LENGTH, head_count, HEAD_DIM)
        value_heads = seq_values.reshape(LENGTH, head_count, HEAD_DIM)
        usable = (positions < length)[None, None, :]
        key_grad = jnp.zeros((LENGTH, head_count, HEAD_DIM), jnp.float32)
        value_grad = jnp.zeros((LENGTH, head_count, HEAD_DIM), jnp.float32)
        query_blocks = []
        for block_start in range(0, LENGTH, block_rows):
            block_q = query_heads[block_start : block_start + block_rows]
            block_grad = seq_grad[block_start : block_start + block_rows].reshape(
                block_rows, head_count, HEAD_DIM
            )
            scores = (
                jnp.einsum("qhd,khd->hqk", block_q, key_heads, preferred_element_type=jnp.float32)
                * scaling
            )
            scores = jnp.where(usable, scores, NEGATIVE)
            chances = jnp.exp(scores - seq_totals[:, block_start : block_start + block_rows, None])
            weights = chances.astype(jnp.bfloat16)
            value_grad = value_grad + jnp.einsum(
                "hqk,qhd->khd", weights, block_grad, preferred_element_type=jnp.float32
            )
            grad_weights = jnp.einsum(
                "qhd,khd->hqk", block_grad, value_heads, preferred_element_type=jnp.float32
            )
            inner_sum = jnp.sum(grad_weights * chances, axis=-1, keepdims=True)
            grad_scores = (chances * (grad_weights - inner_sum)).astype(jnp.bfloat16)
            block_query_grad = (
                jnp.einsum(
                    "hqk,khd->qhd", grad_scores, key_heads, preferred_element_type=jnp.float32
                )
                * scaling
            )
            query_blocks.append(block_query_grad.reshape(block_rows, local_width))
            key_grad = (
                key_grad
                + jnp.einsum(
                    "hqk,qhd->khd", grad_scores, block_q, preferred_element_type=jnp.float32
                )
                * scaling
            )
        query_grad = jnp.concatenate(query_blocks, axis=0).astype(jnp.bfloat16)
        return (
            query_grad,
            key_grad.reshape(LENGTH, local_width).astype(jnp.bfloat16),
            value_grad.reshape(LENGTH, local_width).astype(jnp.bfloat16),
        )

    grad_shaped = grad_context.reshape(seq_count, LENGTH, local_width)
    query_grads, key_grads, value_grads = lax.map(
        backward_seq, (shaped[0], shaped[1], shaped[2], lengths, grad_shaped, log_totals)
    )
    query_grads = query_grads.reshape(seq_count * LENGTH, local_width)
    key_grads = key_grads.reshape(seq_count * LENGTH, local_width)
    value_grads = value_grads.reshape(seq_count * LENGTH, local_width)
    qv_bias_grad = jnp.stack(
        [
            jnp.sum(query_grads.astype(jnp.float32), axis=0),
            jnp.sum(value_grads.astype(jnp.float32), axis=0),
        ]
    )
    qkv_weight_grad = jnp.stack(
        [
            contract_rows(gathered, query_grads),
            contract_rows(gathered, key_grads),
            contract_rows(gathered, value_grads),
        ]
    )
    part_query = lax.slice_in_dim(query_grads, 0, lax.axis_size("tensor") * tok_rows, axis=0)
    input_grad = (
        grad_first
        + lax.psum_scatter(
            (
                contract_cols(part_query, qkv_back[0])
                + contract_cols(key_grads, qkv_back[1])
                + contract_cols(value_grads, qkv_back[2])
            ).astype(jnp.bfloat16),
            "tensor",
            scatter_dimension=0,
            tiled=True,
        ).astype(jnp.float32)
    ).astype(jnp.bfloat16)
    qkv_grad_own, out_grad_own, up_grad_own, down_grad_own = (
        lax.psum_scatter(qkv_weight_grad, "dp", scatter_dimension=1, tiled=True),
        lax.psum_scatter(out_weight_grad, "dp", scatter_dimension=1, tiled=True),
        lax.psum_scatter(up_weight_grad, "dp", scatter_dimension=0, tiled=True),
        lax.psum_scatter(down_weight_grad, "dp", scatter_dimension=1, tiled=True),
    )
    qv_bias_total, up_bias_total = lax.psum((qv_bias_grad, up_bias_grad), "dp")
    (
        out_bias_total,
        down_bias_total,
        gain_one_total,
        shift_one_total,
        gain_two_total,
        shift_two_total,
    ) = lax.psum(
        (
            out_bias_grad,
            down_bias_grad,
            gain_one_grad,
            shift_one_grad,
            gain_two_grad,
            shift_two_grad,
        ),
        ("dp", "tensor"),
    )
    return (
        layer_output,
        input_grad,
        qkv_grad_own,
        qv_bias_total,
        out_grad_own,
        out_bias_total,
        up_grad_own,
        up_bias_total,
        down_grad_own,
        down_bias_total,
        gain_one_total,
        shift_one_total,
        gain_two_total,
        shift_two_total,
    )


def solution(mesh):
    return jax.shard_map(
        per_device,
        mesh=mesh,
        in_specs=(
            P(("dp", "tensor"), None),
            P("dp"),
            P(None, "dp", "tensor"),
            P(None, "tensor"),
            P("tensor", "dp"),
            P(),
            P("dp", "tensor"),
            P("tensor"),
            P("tensor", "dp"),
            P(),
            P(),
            P(),
            P(),
            P(),
            P(("dp", "tensor"), None),
        ),
        out_specs=(
            P(("dp", "tensor"), None),
            P(("dp", "tensor"), None),
            P(None, "dp", "tensor"),
            P(None, "tensor"),
            P("tensor", "dp"),
            P(),
            P("dp", "tensor"),
            P("tensor"),
            P("tensor", "dp"),
            P(),
            P(),
            P(),
            P(),
            P(),
        ),
        check_vma=False,
    )
```

profile of v0, /device:TPU:0, one launch (start us, length us, event | category | flops | bytes accessed | tf_op | source)
XLA Modules:
  0.0 1038.2 jit_solution(9922317103957784277)
XLA Ops:
  9.4 0.8 slice_reduce_fusion
  10.1 49.1 %all_gather.26 = bf16[384,768]{0,1:T(8,128)(2,1)} all-gather(bf16[384,48]{0,1:T(8,128)(2,1)} %param.19), channel_id=1, replica_groups=mesh['dp'=16,'tensor'=2] {'dp'}, dimensions={1}, use_global_device_ids=true | all-gather | bytes 626688 | tf_op jit(solution)/shard_map/all_gather | solution.py:64
  59.2 25.9 %all-gather.10.cloned.1.call-done = bf16[3,768,384]{2,1,0:T(8,128)(2,1)} async-done(((bf16[3,48,384]{2,1,0:T(8,128)(2,1)}), bf16[3,768,384]{2,1,0:T(8,128)(2,1)}) %all-gather.10.cloned.1.call-update) | async-done | bytes 1769488 | tf_op jit(solution)/shard_map/all_gather | solution.py:63
  85.1 2.4 add_convert_fusion.5
  87.6 2.2 convolution_convert_fusion.1
  89.8 1.8 fusion.56
  91.6 4.9 fusion.18
  96.6 5.6 fusion
  102.2 1.9 add_convert_fusion.6
  104.2 3.8 fusion.30
  108.0 3.8 fusion.29
  112.5 2.7 fusion.34
  115.9 9.2 reduce-scatter.8.cloned.1.call-done
  125.1 1.7 fusion.53
  127.1 1.2 fusion.26
  129.2 62.5 %all-gather.14.cloned.1.call-done = bf16[768,1536]{1,0:T(8,128)(2,1)} async-done(((bf16[48,1536]{1,0:T(8,128)(2,1)}), bf16[768,1536]{1,0:T(8,128)(2,1)}) %all-gather.14.cloned.1.call-update) | async-done | bytes 2359312 | tf_op jit(solution)/shard_map/all_gather | solution.py:65
  191.6 10.7 %all-gather.12.cloned.1.call-done = bf16[1024,768]{1,0:T(8,128)(2,1)} async-done(((bf16[512,768]{1,0:T(8,128)(2,1)}), bf16[1024,768]{1,0:T(8,128)(2,1)}) %all-gather.12.cloned.1.call-update) | async-done | bytes 1572880 | tf_op jit(solution)/shard_map/all_gather | solution.py:117
  202.3 19.9 %multiply_convert_fusion.2 = (bf16[1024,1536]{1,0:T(8,128)(2,1)}, f32[1024,1536]{1,0:T(8,128)}, f32[1024,1536]{1,0:T(8,128)}) fusion(f32[1536]{0:T(1024)S(1)} %copy-done.44, bf16[1024,768]{1,0:T(8,128)(2,1)} %all-gather.12.cloned.1.call-done, bf16[768,1536]{1,0:T(8,128)(2,1)} %all-gather.14.cloned.1.call-done), kind=kOutput, calls=%fused_computation.24 | convolution fusion | flops 2519728128 | bytes 19666944 | tf_op jit(solution)/shard_map/dot_general | solution.py:23
  222.2 46.7 %all-gather.16.cloned.1.call-done = bf16[1536,768]{0,1:T(8,128)(2,1)} async-done(((bf16[1536,48]{0,1:T(8,128)(2,1)}), bf16[1536,768]{0,1:T(8,128)(2,1)}) %all-gather.16.cloned.1.call-update) | async-done | bytes 2359312 | tf_op jit(solution)/shard_map/all_gather | solution.py:66
  268.8 6.9 fusion.57
  275.8 9.8 reduce-scatter.10.cloned.1.call-done
  285.6 2.0 fusion.51
  288.7 1.6 fusion.50
  290.3 1.1 convert_reduce_fusion.2
  291.5 11.1 %all-gather.18.cloned.1.call-done = bf16[1024,768]{1,0:T(8,128)(2,1)} async-done(((bf16[512,768]{1,0:T(8,128)(2,1)}), bf16[1024,768]{1,0:T(8,128)(2,1)}) %all-gather.18.cloned.1.call-update) | async-done | bytes 1572880 | tf_op jit(solution)/shard_map/all_gather | solution.py:132
  302.5 10.9 %convert_reduce_fusion = (f32[1536]{0:T(1024)}, bf16[1024,1536]{1,0:T(8,128)(2,1)S(1)}) fusion(f32[1024,1536]{1,0:T(8,128)} %get-tuple-element.135, f32[1024,1536]{1,0:T(8,128)} %get-tuple-element.146, f32[1536]{0:T(1024)S(1)} %copy-done.44, bf16[1024,768]{1,0:T(8,128)(2,1)} %all-gather.18.cloned.1.call-done, ...), kind=kOutput, calls=%fused_computation.20 | convolution fusion | flops 2442656256 | bytes 19673088 | tf_op jit(solution)/shard_map/dot_general | solution.py:33
  313.5 1.6 copy-done.17
  315.1 4.4 fusion.58
  319.5 12.2 %reduce-scatter.12.cloned.1.call-done = f32[512,768]{1,0:T(8,128)} async-done(((f32[1024,768]{1,0:T(8,128)}), f32[512,768]{1,0:T(8,128)}) %reduce-scatter.12.cloned.1.call-update) | async-done | bytes 1572880 | tf_op jit(solution)/shard_map/reduce_scatter | solution.py:140
  331.7 2.8 multiply_reduce_fusion.2
  335.2 1.1 copy-done.2
  336.3 1.7 convert_reduce_fusion.3
  338.5 10.6 %all-gather.20.cloned.1.call-done = bf16[1024,768]{1,0:T(8,128)(2,1)} async-done(((bf16[512,768]{1,0:T(8,128)(2,1)}), bf16[1024,768]{1,0:T(8,128)(2,1)}) %all-gather.20.cloned.1.call-update) | async-done | bytes 1572880 | tf_op jit(solution)/shard_map/all_gather | solution.py:147
  349.1 2.2 convolution_convert_fusion
  351.4 6.4 fusion.59
  357.9 7.3 fusion.5
  365.1 18.9 %multiply_reduce_fusion.1 = (f32[6,512]{1,0:T(8,128)S(1)}, f32[6,512]{1,0:T(8,128)S(1)}, f32[6,512,1024]{2,1,0:T(8,128)}) fusion(f32[6,512]{1,0:T(8,128)S(1)} %get-tuple-element.151, f32[6,512,1024]{2,1,0:T(8,128)} %copy-done.1, pred[1024]{0:T(1024)(128)(4,1)S(1)} %iota_compare_fusion, f32[6,512,1024]{2,1,0:T(8,128)} %fusion.59, ...), kind=kOutput, calls=%fused_computation.4 | convolution fusion | flops 434104320 | bytes 51561472 | tf_op jit(solution)/shard_map/while/body/eval_jaxpr/qhd,khd->hqk/dot_general | solution.py:175
  384.1 17.3 %multiply_convert_fusion.1 = (bf16[6,512,1024]{2,1,0:T(8,128)(2,1)S(1)}, bf16[6,512,1024]{2,1,0:T(8,128)(2,1)S(1)}) fusion(f32[6,512,1024]{2,1,0:T(8,128)} %get-tuple-element.147, f32[6,512]{1,0:T(8,128)S(1)} %get-tuple-element.107, f32[6,512]{1,0:T(8,128)S(1)} %get-tuple-element.151, f32[6,512,1024]{2,1,0:T(8,128)} %copy-done.1, ...), kind=kLoop, calls=%fused_computation.3 | loop fusion | flops 37748736 | bytes 62964736 | tf_op jit(solution)/shard_map/while/body/eval_jaxpr/convert_element_type | solution.py:179
  401.4 2.0 fusion.27
  403.5 1.2 fusion.60
  405.0 7.2 convert_reduce_fusion.4
  412.2 2.0 fusion.28
  414.3 1.3 multiply_convert_fusion.3
  415.9 1.0 fusion.32
  416.9 1.0 fusion.31
  417.9 2.2 add_convert_fusion.1
  420.2 2.3 convolution_bitcast_fusion.2
  422.5 0.8 convolution_bitcast_fusion
  423.3 0.8 convolution_bitcast_fusion.1
  424.3 4.1 copy.30
  428.5 1.4 copy-done.43
  429.9 6.3 fusion.62
  436.3 1.8 copy-done.18
  438.1 5.8 fusion.61
  444.0 0.8 copy-done.25
  445.0 3.5 fusion.33
  449.8 43.9 %all-reduce.1 = (f32[768]{0:T(1024)}, f32[768]{0:T(1024)}, f32[768]{0:T(1024)}, f32[768]{0:T(1024)}, f32[768]{0:T(1024)}, /*index=5*/f32[768]{0:T(1024)}) all-reduce(f32[768]{0:T(1024)S(1)} %copy-done.30, f32[768]{0:T(1024)S(1)} %get-tuple-element.121, f32[768]{0:T(1024)S(1)} %copy-done.32, ...), channel_id=1, replica_groups=mesh['dp'=16,'tensor'=2] {'dp','tensor'}, use_global_device_ids=true, to_apply=%region_24.25 | all-reduce | flops 4608 | bytes 36864 | tf_op jit(solution)/shard_map/psum | solution.py:249
  494.0 76.4 %all-reduce.2 = (f32[2,384]{1,0:T(2,128)}, f32[1536]{0:T(1024)}) all-reduce(f32[2,384]{1,0:T(2,128)S(1)} %pad_maximum_fusion.7, f32[1536]{0:T(1024)S(1)} %copy-done.34), channel_id=1, replica_groups=mesh['dp'=16,'tensor'=2] {'dp'}, use_global_device_ids=true, to_apply=%region_21.22 | all-reduce | flops 2304 | bytes 18432 | tf_op jit(solution)/shard_map/psum | solution.py:241
  570.5 2.3 add_convert_fusion.2
  572.7 45.6 %all-reduce.5.cloned.1.call-done = f32[3,768,384]{2,0,1:T(4,128)} async-done(((f32[3,768,384]{2,0,1:T(4,128)}), f32[3,768,384]{2,0,1:T(4,128)}) %all-reduce.5.cloned.1.call-update) | async-done | bytes 3538960
  618.3 1.0 constant_dynamic-slice_fusion
  620.1 141.2 %reduce-scatter.20.cloned.1.call-done = f32[1536,48]{0,1:T(8,128)} async-done(((f32[1536,768]{0,1:T(8,128)}), f32[1536,48]{0,1:T(8,128)}) %reduce-scatter.20.cloned.1.call-update) | async-done | bytes 294928 | tf_op jit(solution)/shard_map/reduce_scatter | solution.py:239
  761.2 141.7 %reduce-scatter.18.cloned.1.call-done = f32[48,1536]{1,0:T(8,128)} async-done(((f32[768,1536]{1,0:T(8,128)}), f32[48,1536]{1,0:T(8,128)}) %reduce-scatter.18.cloned.1.call-update) | async-done | bytes 294928 | tf_op jit(solution)/shard_map/reduce_scatter | solution.py:238
  902.9 128.6 %reduce-scatter.16.cloned.1.call-done = f32[384,48]{0,1:T(8,128)} async-done(((f32[384,768]{0,1:T(8,128)}), f32[384,48]{0,1:T(8,128)}) %reduce-scatter.16.cloned.1.call-update) | async-done | bytes 73744 | tf_op jit(solution)/shard_map/reduce_scatter | solution.py:237
  (144 shorter events, 9.4 us)
Async XLA Ops:
  7.2 52.0 %all-gather.8.cloned.1.call-start = ((), (), s32[]{:S(2)}) async-start(), calls=%async_computation.7 | async-start | bytes 2359296 | tf_op jit(solution)/shard_map/all_gather | solution.py:68
  7.9 77.2 %all-gather.10.cloned.1.call-start = ((), (), s32[]{:S(2)}) async-start(), calls=%async_computation.8 | async-start | bytes 1880064 | tf_op jit(solution)/shard_map/all_gather | solution.py:63
  8.7 116.4 %reduce-scatter.8.cloned.1.call-start = ((), (), s32[]{:S(2)}) async-start(), calls=%async_computation.9 | async-start | bytes 4718592 | tf_op jit(solution)/shard_map/reduce_scatter | solution.py:111
  59.2 28.3 %copy-start.40 = (bf16[1024,768]{1,0:T(8,128)(2,1)S(1)}, bf16[1024,768]{1,0:T(8,128)(2,1)}, u32[]{:S(2)}) copy-start(bf16[1024,768]{1,0:T(8,128)(2,1)} %all-gather.8.cloned.1.call-done) | copy-start | bytes 4718596
  87.6 4.1 copy-start.6
  87.6 4.1 copy-start.8
  89.8 1.9 copy-start.4
  91.6 16.3 %copy-start = (f32[6,512,1024]{2,1,0:T(8,128)}, f32[6,512,1024]{2,1,0:T(8,128)S(1)}, u32[]{:S(2)}) copy-start(f32[6,512,1024]{2,1,0:T(8,128)S(1)} %fusion.56) | copy-start | bytes 37748740
  96.5 7.6 copy-start.1
  96.6 5.7 copy-start.41
  104.1 3.8 copy-start.19
  107.9 3.8 copy-start.24
  108.0 4.5 copy-start.21
  111.8 0.7 copy-start.26
  112.5 12.6 %copy-start.16 = (bf16[512,768]{1,0:T(8,128)(2,1)S(1)}, bf16[512,768]{1,0:T(8,128)(2,1)}, u32[]{:S(2)}) copy-start(bf16[512,768]{1,0:T(8,128)(2,1)} %param.15) | copy-start | bytes 2359300
  112.5 12.6 %copy-start.37 = (f32[768]{0:T(1024)S(1)}, f32[768]{0:T(1024)}, u32[]{:S(2)}) copy-start(f32[768]{0:T(1024)} %param.20) | copy-start | bytes 9220
  115.3 11.8 %copy-start.28 = (f32[768]{0:T(1024)S(1)}, f32[768]{0:T(1024)}, u32[]{:S(2)}) copy-start(f32[768]{0:T(1024)} %param.25) | copy-start | bytes 9220
  115.3 11.8 %copy-start.31 = (f32[768]{0:T(1024)S(1)}, f32[768]{0:T(1024)}, u32[]{:S(2)}) copy-start(f32[768]{0:T(1024)} %param.26) | copy-start | bytes 9220
  115.3 76.3 %all-gather.14.cloned.1.call-start = ((), (), s32[]{:S(2)}) async-start(), calls=%async_computation.11 | async-start | bytes 2506752 | tf_op jit(solution)/shard_map/all_gather | solution.py:65
  115.9 86.4 %all-gather.12.cloned.1.call-start = ((), (), s32[]{:S(2)}) async-start(), calls=%async_computation.10 | async-start | bytes 2359296 | tf_op jit(solution)/shard_map/all_gather | solution.py:117
  126.8 75.5 %copy-start.44 = (f32[1536]{0:T(1024)S(1)}, f32[1536]{0:T(1024)}, u32[]{:S(2)}) copy-start(f32[1536]{0:T(1024)} %param.22) | copy-start | bytes 18436
  128.4 140.5 %all-gather.16.cloned.1.call-start = ((), (), s32[]{:S(2)}) async-start(), calls=%async_computation.12 | async-start | bytes 2506752 | tf_op jit(solution)/shard_map/all_gather | solution.py:66
  128.9 156.7 %reduce-scatter.10.cloned.1.call-start = ((), (), s32[]{:S(2)}) async-start(), calls=%async_computation.13 | async-start | bytes 4718592 | tf_op jit(solution)/shard_map/reduce_scatter | solution.py:122
  275.7 9.9 copy-start.38
  275.7 12.2 %copy-start.14 = (bf16[512,768]{1,0:T(8,128)(2,1)S(1)}, bf16[512,768]{1,0:T(8,128)(2,1)}, u32[]{:S(2)}) copy-start(bf16[512,768]{1,0:T(8,128)(2,1)} %param.29) | copy-start | bytes 2359300
  275.8 12.2 %copy-start.29 = (f32[768]{0:T(1024)S(1)}, f32[768]{0:T(1024)}, u32[]{:S(2)}) copy-start(f32[768]{0:T(1024)} %param.27) | copy-start | bytes 9220
  275.8 26.8 %all-gather.18.cloned.1.call-start = ((), (), s32[]{:S(2)}) async-start(), calls=%async_computation.14 | async-start | bytes 2359296 | tf_op jit(solution)/shard_map/all_gather | solution.py:132
  287.6 1.1 copy-start.15
  287.6 1.1 copy-start.35
  291.4 40.3 %reduce-scatter.12.cloned.1.call-start = ((), (), s32[]{:S(2)}) async-start(), calls=%async_computation.15 | async-start | bytes 4718592 | tf_op jit(solution)/shard_map/reduce_scatter | solution.py:140
  302.5 12.5 %copy-start.39 = (bf16[768,1536]{1,0:T(8,128)(2,1)S(1)}, bf16[768,1536]{1,0:T(8,128)(2,1)}, u32[]{:S(2)}) copy-start(bf16[768,1536]{1,0:T(8,128)(2,1)} %all-gather.14.cloned.1.call-done) | copy-start | bytes 7077892
  313.5 1.6 copy-start.17
  319.5 29.7 %all-gather.20.cloned.1.call-start = ((), (), s32[]{:S(2)}) async-start(), calls=%async_computation.16 | async-start | bytes 2359296 | tf_op jit(solution)/shard_map/all_gather | solution.py:147
  334.5 14.6 %copy-start.22 = (bf16[384,768]{0,1:T(8,128)(2,1)S(1)}, bf16[384,768]{0,1:T(8,128)(2,1)}, u32[]{:S(2)}) copy-start(bf16[384,768]{0,1:T(8,128)(2,1)} %all_gather.26) | copy-start | bytes 1769476
  335.2 1.1 copy-start.2
  338.0 13.4 %copy-start.20 = (bf16[1024,384]{0,1:T(8,128)(2,1)S(1)}, bf16[1024,384]{0,1:T(8,128)(2,1)}, u32[]{:S(2)}) copy-start(bf16[1024,384]{0,1:T(8,128)(2,1)} %copy-done.19) | copy-start | bytes 2359300
  338.0 232.5 %reduce-scatter.14.cloned.1.call-start = ((), (), s32[]{:S(2)}) async-start(), calls=%async_computation.17 | async-start | bytes 2359296 | tf_op jit(solution)/shard_map/reduce_scatter | solution.py:224
  384.1 17.3 %copy-start.5 = (bf16[1024,384]{0,1:T(8,128)(2,1)S(1)}, bf16[1024,384]{0,1:T(8,128)(2,1)}, u32[]{:S(2)}) copy-start(bf16[1024,384]{0,1:T(8,128)(2,1)} %copy-done.4) | copy-start | bytes 2359300
  401.4 2.0 copy-start.9
  403.5 16.7 %copy-start.10 = (bf16[6,64,512]{2,1,0:T(8,128)(2,1)}, bf16[6,64,512]{2,1,0:T(8,128)(2,1)S(1)}, u32[]{:S(2)}) copy-start(bf16[6,64,512]{2,1,0:T(8,128)(2,1)S(1)} %fusion.27) | copy-start | bytes 1179652
  403.5 1.6 copy-start.46
  412.2 2.0 copy-start.7
  414.3 6.0 copy-start.12
  414.3 1.6 copy-start.23
  420.2 198.2 %all-reduce.5.cloned.1.call-start = ((), (), s32[]{:S(2)}) async-start(), calls=%async_computation.21 | async-start | bytes 9437184
  420.2 2.3 copy-start.42
  428.4 1.5 copy-start.43
  428.4 332.8 %reduce-scatter.20.cloned.1.call-start = ((), (), s32[]{:S(2)}) async-start(), calls=%async_computation.20 | async-start | bytes 5013504 | tf_op jit(solution)/shard_map/reduce_scatter | solution.py:239
  436.2 1.9 copy-start.18
  436.2 466.7 %reduce-scatter.18.cloned.1.call-start = ((), (), s32[]{:S(2)}) async-start(), calls=%async_computation.19 | async-start | bytes 5013504 | tf_op jit(solution)/shard_map/reduce_scatter | solution.py:238
  443.9 1.0 copy-start.25
  443.9 1.1 copy-start.27
  443.9 4.6 copy-start.45
  443.9 5.9 copy-start.30
  443.9 5.9 copy-start.32
  443.9 5.9 copy-start.33
  443.9 49.8 %copy-start.36 = (f32[6,64]{1,0:T(8,128)S(1)}, f32[6,64]{1,0:T(8,128)}, u32[]{:S(2)}) copy-start(f32[6,64]{1,0:T(8,128)} %get-tuple-element.148) | copy-start | bytes 4612
  443.9 49.9 %copy-start.11 = (bf16[6,64,512]{2,1,0:T(8,128)(2,1)S(1)}, bf16[6,64,512]{2,1,0:T(8,128)(2,1)}, u32[]{:S(2)}) copy-start(bf16[6,64,512]{2,1,0:T(8,128)(2,1)} %copy-done.10) | copy-start | bytes 1179652
  444.0 49.8 %copy-start.13 = (bf16[6,64,512]{2,1,0:T(8,128)(2,1)S(1)}, bf16[6,64,512]{2,1,0:T(8,128)(2,1)}, u32[]{:S(2)}) copy-start(bf16[6,64,512]{2,1,0:T(8,128)(2,1)} %copy-done.12) | copy-start | bytes 1179652
  444.0 50.0 %copy-start.34 = (f32[1536]{0:T(1024)S(1)}, f32[1536]{0:T(1024)}, u32[]{:S(2)}) copy-start(f32[1536]{0:T(1024)} %get-tuple-element.125) | copy-start | bytes 18436
  444.0 126.5 %copy-start.3 = (f32[512,768]{1,0:T(8,128)S(1)}, f32[512,768]{1,0:T(8,128)}, u32[]{:S(2)}) copy-start(f32[512,768]{1,0:T(8,128)} %copy-done.2) | copy-start | bytes 4718596
  444.0 587.5 %reduce-scatter.16.cloned.1.call-start = ((), (), s32[]{:S(2)}) async-start(), calls=%async_computation.18 | async-start | bytes 1253376 | tf_op jit(solution)/shard_map/reduce_scatter | solution.py:237
Sparse Core Ops, SparseCore 0:
  9.6 12.4 all-gather.7
  24.8 60.2 all-gather.9
  115.4 9.6 reduce-scatter.7
  128.1 63.4 all-gather.13
  193.7 8.6 all-gather.11
  205.3 63.4 all-gather.15
  275.9 9.7 reduce-scatter.9
  291.5 10.9 all-gather.17
  319.6 12.0 reduce-scatter.11
  338.1 10.9 all-gather.19
  420.3 10.2 reduce-scatter.13
  436.1 182.1 all-reduce.4
  624.9 136.2 reduce-scatter.19
  766.8 136.0 reduce-scatter.17
  908.8 122.6 reduce-scatter.15
where the time goes:
time: 1050 us; the launch traced here: 1040 us
  waiting for transfers between devices  658 us (63%)
  blocking collectives  169 us (16%)
  matrix products  138 us (13%)
  other arithmetic  39.6 us (4%)
  between operations  16.1 us (2%)
  local copies, waits for them, and re-layouts  15.8 us (2%)
    reduce_scatter x1, waiting for transfers between devices, per_device(): lax.psum_scatter(up_weight_grad, 'dp', scatter_dimension=0, tiled=True)  142 us
    reduce_scatter x1, waiting for transfers between devices, per_device(): lax.psum_scatter(down_weight_grad, 'dp', scatter_dimension=1, tiled=True)  141 us
    reduce_scatter x1, waiting for transfers between devices, per_device(): lax.psum_scatter(out_weight_grad, 'dp', scatter_dimension=1, tiled=True)  129 us
    psum x1, blocking collectives, per_device(): qv_bias_total, up_bias_total = lax.psum((qv_bias_grad, up_bias_grad), 'dp')  76.4 us
    all_gather x1, waiting for transfers between devices, per_device(): lax.all_gather(up_weight, 'dp', axis=0, tiled=True)  62.5 us
    all_gather x1, blocking collectives, per_device(): lax.all_gather(out_weight, 'dp', axis=1, tiled=True)  49.1 us
    unnamed x16, waiting for transfers between devices  48.2 us
    all_gather x1, waiting for transfers between devices, per_device(): lax.all_gather(down_weight, 'dp', axis=1, tiled=True)  46.7 us
  transfers between devices with their start and end apart: 15, of which 13 were waited for; matrix products, arithmetic and copies ran while one was open for 5% of the time, Pallas kernels for 0%

commit v1 on v0

--- a/solution.py
+++ b/solution.py
@@ -7,6 +7,24 @@
 LENGTH = 1024
 EPSILON = 1e-05
 NEGATIVE = -1e30
+
+
+def ring_gather(value, axis, dim):
+    ways, here, hop = (lax.axis_size(axis), lax.axis_index(axis), value.shape[dim])
+    shape = [n * ways if d == dim else n for d, n in enumerate(value.shape)]
+    full = lax.dynamic_update_slice_in_dim(
+        jnp.zeros(shape, value.dtype), value, here * hop, axis=dim
+    )
+    going_up = going_down = value
+    for far in range(1, ways // 2 + 1):
+        going_up = lax.ppermute(going_up, axis, [(d, (d + 1) % ways) for d in range(ways)])
+        full = lax.dynamic_update_slice_in_dim(full, going_up, (here - far) % ways * hop, axis=dim)
+        if 2 * far < ways:
+            going_down = lax.ppermute(going_down, axis, [(d, (d - 1) % ways) for d in range(ways)])
+            full = lax.dynamic_update_slice_in_dim(
+                full, going_down, (here + far) % ways * hop, axis=dim
+            )
+    return full
 
 
 def layer_norm(values, norm_gain, norm_shift):
@@ -60,7 +78,7 @@
     scaling = HEAD_DIM ** (-0.5)
     positions = jnp.arange(LENGTH)
     qkv_full, out_full, up_full, down_full = (
-        lax.all_gather(qkv_weight, "dp", axis=1, tiled=True),
+        ring_gather(qkv_weight, "dp", 1),
         lax.all_gather(out_weight, "dp", axis=1, tiled=True),
         lax.all_gather(up_weight, "dp", axis=0, tiled=True),
         lax.all_gather(down_weight, "dp", axis=1, tiled=True),

time: 1050 us -> 943 us (0.90)
  waiting for transfers between devices: 658 us -> 523 us
  starting transfers between devices: 1.19 us -> 37.1 us
    reduce_scatter x1, waiting for transfers between devices: 141 us -> 8.11 us  [per_device(): lax.psum_scatter(down_weight_grad, 'dp', scatter_dimension=1, tiled=True)]
    ppermute x0 -> x15, starting transfers between devices: none -> 35.9 us  [the longest x7 33.7 us: ring_gather(): lax.ppermute(going_down, axis, [(d, (d - 1) % ways) for d in range(ways)])]
    ppermute x0 -> x15, waiting for transfers between devices: none -> 29.6 us  [the longest x8 17.2 us: ring_gather(): lax.ppermute(going_up, axis, [(d, (d + 1) % ways) for d in range(ways)])]
    all_gather x1 -> x0, waiting for transfers between devices: 25.9 us -> none  [per_device(): lax.all_gather(qkv_weight, 'dp', axis=1, tiled=True)]
    all_gather x1, waiting for transfers between devices: 62.5 us -> 51 us  [per_device(): lax.all_gather(up_weight, 'dp', axis=0, tiled=True)]
    unnamed x16 -> x15, waiting for transfers between devices: 48.2 us -> 57.1 us
  transfers between devices with their start and end apart: 15 -> 29, of which waited for: 13 -> 24; matrix products, arithmetic and copies ran while one was open for 5% -> 6% of each run, Pallas kernels for 0% -> 0%
where the time goes in v1:
time: 943 us; the launch traced here: 939 us
  waiting for transfers between devices  523 us (55%)
  blocking collectives  168 us (18%)
  matrix products  137 us (15%)
  other arithmetic  39.7 us (4%)
  starting transfers between devices  37.1 us (4%)
  between operations  18.3 us (2%)
  local copies, waits for them, and re-layouts  16.4 us (2%)
    reduce_scatter x1, waiting for transfers between devices, per_device(): lax.psum_scatter(up_weight_grad, 'dp', scatter_dimension=0, tiled=True)  142 us
    reduce_scatter x1, waiting for transfers between devices, per_device(): lax.psum_scatter(out_weight_grad, 'dp', scatter_dimension=1, tiled=True)  129 us
    psum x1, blocking collectives, per_device(): qv_bias_total, up_bias_total = lax.psum((qv_bias_grad, up_bias_grad), 'dp')  76.5 us
    unnamed x15, waiting for transfers between devices  57.1 us
    all_gather x1, waiting for transfers between devices, per_device(): lax.all_gather(up_weight, 'dp', axis=0, tiled=True)  51 us
    all_gather x1, blocking collectives, per_device(): lax.all_gather(out_weight, 'dp', axis=1, tiled=True)  47.5 us
    all_gather x1, waiting for transfers between devices, per_device(): lax.all_gather(down_weight, 'dp', axis=1, tiled=True)  46.9 us
    psum x1, blocking collectives, per_device(): lax.psum((out_bias_grad, down_bias_grad, gain_one_grad, shift_one_grad, g...  43.9 us
  transfers between devices with their start and end apart: 29, of which 24 were waited for; matrix products, arithmetic and copies ran while one was open for 6% of the time, Pallas kernels for 0%

profile of v1, /device:TPU:0, one launch (start us, length us, event | category | flops | bytes accessed | tf_op | source)
XLA Modules:
  0.0 939.5 jit_solution(11230341049054929111)
XLA Ops:
  8.1 7.0 collective-permute-start.1
  16.8 47.5 %all_gather.22 = bf16[384,768]{0,1:T(8,128)(2,1)} all-gather(bf16[384,48]{0,1:T(8,128)(2,1)} %param.19), channel_id=1, replica_groups=mesh['dp'=16,'tensor'=2] {'dp'}, dimensions={1}, use_global_device_ids=true | all-gather | bytes 626688 | tf_op jit(solution)/shard_map/all_gather | solution.py:82
  64.7 2.0 collective-permute-start.2
  66.7 3.8 collective-permute-done.3
  70.6 2.4 collective-permute-start.5
  73.2 2.2 collective-permute-done.5
  75.4 6.1 collective-permute-start.7
  81.6 2.1 collective-permute-done.7
  83.8 6.0 collective-permute-start.9
  90.0 2.1 collective-permute-done.9
  92.1 6.1 collective-permute-start.11
  98.4 2.2 collective-permute-done.11
  100.6 6.0 collective-permute-start.13
  106.8 8.3 collective-permute-done.12
  115.3 8.3 collective-permute-done.14
  123.6 2.9 fusion.26
  127.5 1.8 fusion.58
  129.3 4.9 fusion.18
  134.3 5.6 fusion
  139.9 1.9 add_convert_fusion.6
  141.9 3.8 fusion.31
  145.7 3.8 fusion.30
  150.2 2.7 fusion.36
  153.6 6.3 reduce-scatter.8.cloned.1.call-done
  159.9 1.7 fusion.55
  164.0 51.0 %all-gather.11.cloned.1.call-done = bf16[768,1536]{1,0:T(8,128)(2,1)} async-done(((bf16[48,1536]{1,0:T(8,128)(2,1)}), bf16[768,1536]{1,0:T(8,128)(2,1)}) %all-gather.11.cloned.1.call-update) | async-done | bytes 2359312 | tf_op jit(solution)/shard_map/all_gather | solution.py:83
  215.0 10.0 %all-gather.9.cloned.1.call-done = bf16[1024,768]{1,0:T(8,128)(2,1)} async-done(((bf16[512,768]{1,0:T(8,128)(2,1)}), bf16[1024,768]{1,0:T(8,128)(2,1)}) %all-gather.9.cloned.1.call-update) | async-done | bytes 1572880 | tf_op jit(solution)/shard_map/all_gather | solution.py:135
  225.1 19.9 %multiply_convert_fusion.2 = (bf16[1024,1536]{1,0:T(8,128)(2,1)}, f32[1024,1536]{1,0:T(8,128)}, f32[1024,1536]{1,0:T(8,128)}) fusion(f32[1536]{0:T(1024)S(1)} %copy-done.46, bf16[1024,768]{1,0:T(8,128)(2,1)} %all-gather.9.cloned.1.call-done, bf16[768,1536]{1,0:T(8,128)(2,1)} %all-gather.11.cloned.1.call-done), kind=kOutput, calls=%fused_computation.24 | convolution fusion | flops 2519728128 | bytes 19666944 | tf_op jit(solution)/shard_map/dot_general | solution.py:41
  245.0 46.9 %all-gather.13.cloned.1.call-done = bf16[1536,768]{0,1:T(8,128)(2,1)} async-done(((bf16[1536,48]{0,1:T(8,128)(2,1)}), bf16[1536,768]{0,1:T(8,128)(2,1)}) %all-gather.13.cloned.1.call-update) | async-done | bytes 2359312 | tf_op jit(solution)/shard_map/all_gather | solution.py:84
  291.9 6.9 fusion.59
  298.9 9.2 reduce-scatter.10.cloned.1.call-done
  308.1 2.0 fusion.53
  311.2 1.6 fusion.52
  314.0 10.9 %all-gather.15.cloned.1.call-done = bf16[1024,768]{1,0:T(8,128)(2,1)} async-done(((bf16[512,768]{1,0:T(8,128)(2,1)}), bf16[1024,768]{1,0:T(8,128)(2,1)}) %all-gather.15.cloned.1.call-update) | async-done | bytes 1572880 | tf_op jit(solution)/shard_map/all_gather | solution.py:150
  324.9 10.9 %convert_reduce_fusion = (f32[1536]{0:T(1024)}, bf16[1024,1536]{1,0:T(8,128)(2,1)S(1)}) fusion(f32[1024,1536]{1,0:T(8,128)} %get-tuple-element.135, f32[1024,1536]{1,0:T(8,128)} %get-tuple-element.146, f32[1536]{0:T(1024)S(1)} %copy-done.46, bf16[1024,768]{1,0:T(8,128)(2,1)} %all-gather.15.cloned.1.call-done, ...), kind=kOutput, calls=%fused_computation.20 | convolution fusion | flops 2442656256 | bytes 19673088 | tf_op jit(solution)/shard_map/dot_general | solution.py:51
  335.9 1.7 copy-done.19
  337.5 4.3 fusion.60
  341.9 12.0 %reduce-scatter.12.cloned.1.call-done = f32[512,768]{1,0:T(8,128)} async-done(((f32[1024,768]{1,0:T(8,128)}), f32[512,768]{1,0:T(8,128)}) %reduce-scatter.12.cloned.1.call-update) | async-done | bytes 1572880 | tf_op jit(solution)/shard_map/reduce_scatter | solution.py:158
  354.0 2.8 multiply_reduce_fusion.2
  358.6 1.7 convert_reduce_fusion.3
  360.8 10.7 %all-gather.17.cloned.1.call-done = bf16[1024,768]{1,0:T(8,128)(2,1)} async-done(((bf16[512,768]{1,0:T(8,128)(2,1)}), bf16[1024,768]{1,0:T(8,128)(2,1)}) %all-gather.17.cloned.1.call-update) | async-done | bytes 1572880 | tf_op jit(solution)/shard_map/all_gather | solution.py:165
  371.5 2.2 convolution_convert_fusion
  373.8 6.4 fusion.61
  380.2 7.2 fusion.5
  387.5 19.0 %multiply_reduce_fusion.1 = (f32[6,512]{1,0:T(8,128)S(1)}, f32[6,512]{1,0:T(8,128)S(1)}, f32[6,512,1024]{2,1,0:T(8,128)}) fusion(f32[6,512]{1,0:T(8,128)S(1)} %get-tuple-element.151, f32[6,512,1024]{2,1,0:T(8,128)} %copy-done.1, pred[1024]{0:T(1024)(128)(4,1)S(1)} %iota_compare_fusion, f32[6,512,1024]{2,1,0:T(8,128)} %fusion.61, ...), kind=kOutput, calls=%fused_computation.4 | convolution fusion | flops 434104320 | bytes 51561472 | tf_op jit(solution)/shard_map/while/body/eval_jaxpr/qhd,khd->hqk/dot_general | solution.py:193
  406.5 17.3 %multiply_convert_fusion.1 = (bf16[6,512,1024]{2,1,0:T(8,128)(2,1)S(1)}, bf16[6,512,1024]{2,1,0:T(8,128)(2,1)S(1)}) fusion(f32[6,512,1024]{2,1,0:T(8,128)} %get-tuple-element.147, f32[6,512]{1,0:T(8,128)S(1)} %get-tuple-element.107, f32[6,512]{1,0:T(8,128)S(1)} %get-tuple-element.151, f32[6,512,1024]{2,1,0:T(8,128)} %copy-done.1, ...), kind=kLoop, calls=%fused_computation.3 | loop fusion | flops 37748736 | bytes 62964736 | tf_op jit(solution)/shard_map/while/body/eval_jaxpr/convert_element_type | solution.py:197
  423.8 2.0 fusion.28
  427.4 7.2 convert_reduce_fusion.4
  434.6 2.0 fusion.29
  440.3 2.2 add_convert_fusion.1
  442.6 2.3 convolution_bitcast_fusion.2
  446.7 4.0 copy.30
  450.8 1.4 copy-done.45
  452.2 6.4 fusion.64
  458.7 1.9 copy-done.20
  460.6 5.8 fusion.63
  467.5 3.7 fusion.35
  472.4 43.9 %all-reduce.1 = (f32[768]{0:T(1024)}, f32[768]{0:T(1024)}, f32[768]{0:T(1024)}, f32[768]{0:T(1024)}, f32[768]{0:T(1024)}, /*index=5*/f32[768]{0:T(1024)}) all-reduce(f32[768]{0:T(1024)S(1)} %copy-done.32, f32[768]{0:T(1024)S(1)} %get-tuple-element.121, f32[768]{0:T(1024)S(1)} %copy-done.34, ...), channel_id=1, replica_groups=mesh['dp'=16,'tensor'=2] {'dp','tensor'}, use_global_device_ids=true, to_apply=%region_24.25 | all-reduce | flops 4608 | bytes 36864 | tf_op jit(solution)/shard_map/psum | solution.py:267
  516.6 76.5 %all-reduce.2 = (f32[2,384]{1,0:T(2,128)}, f32[1536]{0:T(1024)}) all-reduce(f32[2,384]{1,0:T(2,128)S(1)} %pad_maximum_fusion.7, f32[1536]{0:T(1024)S(1)} %copy-done.36), channel_id=1, replica_groups=mesh['dp'=16,'tensor'=2] {'dp'}, use_global_device_ids=true, to_apply=%region_21.22 | all-reduce | flops 2304 | bytes 18432 | tf_op jit(solution)/shard_map/psum | solution.py:259
  593.1 2.3 add_convert_fusion.2
  595.4 55.9 %all-reduce.5.cloned.1.call-done = f32[3,768,384]{2,0,1:T(4,128)} async-done(((f32[3,768,384]{2,0,1:T(4,128)}), f32[3,768,384]{2,0,1:T(4,128)}) %all-reduce.5.cloned.1.call-update) | async-done | bytes 3538960
  653.0 8.1 reduce-scatter.20.cloned.1.call-done
  661.1 141.9 %reduce-scatter.18.cloned.1.call-done = f32[48,1536]{1,0:T(8,128)} async-done(((f32[768,1536]{1,0:T(8,128)}), f32[48,1536]{1,0:T(8,128)}) %reduce-scatter.18.cloned.1.call-update) | async-done | bytes 294928 | tf_op jit(solution)/shard_map/reduce_scatter | solution.py:256
  803.0 128.9 %reduce-scatter.16.cloned.1.call-done = f32[384,48]{0,1:T(8,128)} async-done(((f32[384,768]{0,1:T(8,128)}), f32[384,48]{0,1:T(8,128)}) %reduce-scatter.16.cloned.1.call-update) | async-done | bytes 73744 | tf_op jit(solution)/shard_map/reduce_scatter | solution.py:255
  (192 shorter events, 22.5 us)
Async XLA Ops:
  8.0 56.5 %copy-start.29 = (bf16[3,48,384]{2,1,0:T(8,128)(2,1)S(1)}, bf16[3,48,384]{2,1,0:T(8,128)(2,1)}, u32[]{:S(2)}) copy-start(bf16[3,48,384]{2,1,0:T(8,128)(2,1)} %param.17) | copy-start | bytes 331780
  8.0 115.6 %all-gather.7.cloned.1.call-start = ((), (), s32[]{:S(2)}) async-start(), calls=%async_computation.7 | async-start | bytes 2359296 | tf_op jit(solution)/shard_map/all_gather | solution.py:86
  8.1 56.5 %collective-permute-start.1 = (bf16[3,48,384]{2,1,0:T(8,128)(2,1)}, bf16[3,48,384]{2,1,0:T(8,128)(2,1)S(1)}, u32[]{:S(2)}, u32[]{:S(2)}) collective-permute-start(bf16[3,48,384]{2,1,0:T(8,128)(2,1)} %param.17), channel_id=1, source_target_pairs={{0,30},{2,0},{4,2},{6,4},{8,6},{10,8},{12,10},{14,12},{16,14},{18,... | collective-permute-start | bytes 331784 | tf_op jit(solution)/shard_map/ppermute | solution.py:23
  15.1 49.6 %collective-permute-start = (bf16[3,48,384]{2,1,0:T(8,128)(2,1)}, bf16[3,48,384]{2,1,0:T(8,128)(2,1)S(1)}, u32[]{:S(2)}, u32[]{:S(2)}) collective-permute-start(bf16[3,48,384]{2,1,0:T(8,128)(2,1)} %param.17), channel_id=1, source_target_pairs={{0,2},{2,4},{4,6},{6,8},{8,10},{10,12},{12,14},{14,16},{16,18},{18... | collective-permute-start | bytes 331784 | tf_op jit(solution)/shard_map/ppermute | solution.py:20
  15.1 144.8 %reduce-scatter.8.cloned.1.call-start = ((), (), s32[]{:S(2)}) async-start(), calls=%async_computation.8 | async-start | bytes 4718592 | tf_op jit(solution)/shard_map/reduce_scatter | solution.py:129
  64.6 6.0 collective-permute-start.3
  64.7 8.5 collective-permute-start.2
  70.6 4.8 collective-permute-start.5
  73.1 8.5 collective-permute-start.4
  75.4 8.4 collective-permute-start.7
  81.6 8.3 collective-permute-start.6
  83.8 8.3 collective-permute-start.9
  89.9 8.4 collective-permute-start.8
  92.1 8.4 collective-permute-start.11
  98.4 8.3 collective-permute-start.10
  100.6 14.7 %collective-permute-start.13 = (bf16[3,48,384]{2,1,0:T(8,128)(2,1)S(1)}, bf16[3,48,384]{2,1,0:T(8,128)(2,1)S(1)}, u32[]{:S(2)}, u32[]{:S(2)}) collective-permute-start(bf16[3,48,384]{2,1,0:T(8,128)(2,1)S(1)} %collective-permute-done.11), channel_id=1, source_target_pairs={{0,30},{2,0},{4,2},{6,4},{8,6},{10,8},{12,10},{14,12},{16,14},{18,... | collective-permute-start | bytes 331784 | tf_op jit(solution)/shard_map/ppermute | solution.py:23
  106.7 8.3 collective-permute-start.12
  115.1 8.5 collective-permute-start.14
  123.6 3.9 copy-start.6
  123.6 3.0 copy-start.42
  126.6 2.7 copy-start.8
  126.6 2.7 copy-start.10
  129.3 16.3 %copy-start = (f32[6,512,1024]{2,1,0:T(8,128)}, f32[6,512,1024]{2,1,0:T(8,128)S(1)}, u32[]{:S(2)}) copy-start(f32[6,512,1024]{2,1,0:T(8,128)S(1)} %fusion.58) | copy-start | bytes 37748740
  134.2 7.6 copy-start.1
  134.2 5.7 copy-start.43
  141.8 3.8 copy-start.21
  145.6 3.8 copy-start.25
  145.7 4.5 copy-start.23
  150.2 9.7 %copy-start.18 = (bf16[512,768]{1,0:T(8,128)(2,1)S(1)}, bf16[512,768]{1,0:T(8,128)(2,1)}, u32[]{:S(2)}) copy-start(bf16[512,768]{1,0:T(8,128)(2,1)} %param.15) | copy-start | bytes 2359300
  150.2 9.7 %copy-start.39 = (f32[768]{0:T(1024)S(1)}, f32[768]{0:T(1024)}, u32[]{:S(2)}) copy-start(f32[768]{0:T(1024)} %param.20) | copy-start | bytes 9220
  153.0 9.0 copy-start.30
  153.0 9.0 copy-start.33
  153.0 62.1 %all-gather.11.cloned.1.call-start = ((), (), s32[]{:S(2)}) async-start(), calls=%async_computation.10 | async-start | bytes 2506752 | tf_op jit(solution)/shard_map/all_gather | solution.py:83
  153.6 71.5 %all-gather.9.cloned.1.call-start = ((), (), s32[]{:S(2)}) async-start(), calls=%async_computation.9 | async-start | bytes 2359296 | tf_op jit(solution)/shard_map/all_gather | solution.py:135
  161.6 63.5 %copy-start.46 = (f32[1536]{0:T(1024)S(1)}, f32[1536]{0:T(1024)}, u32[]{:S(2)}) copy-start(f32[1536]{0:T(1024)} %param.22) | copy-start | bytes 18436
  163.2 128.7 %all-gather.13.cloned.1.call-start = ((), (), s32[]{:S(2)}) async-start(), calls=%async_computation.11 | async-start | bytes 2506752 | tf_op jit(solution)/shard_map/all_gather | solution.py:84
  163.8 144.3 %reduce-scatter.10.cloned.1.call-start = ((), (), s32[]{:S(2)}) async-start(), calls=%async_computation.12 | async-start | bytes 4718592 | tf_op jit(solution)/shard_map/reduce_scatter | solution.py:140
  298.8 9.3 copy-start.40
  298.8 11.6 %copy-start.16 = (bf16[512,768]{1,0:T(8,128)(2,1)S(1)}, bf16[512,768]{1,0:T(8,128)(2,1)}, u32[]{:S(2)}) copy-start(bf16[512,768]{1,0:T(8,128)(2,1)} %param.29) | copy-start | bytes 2359300
  298.8 11.6 %copy-start.31 = (f32[768]{0:T(1024)S(1)}, f32[768]{0:T(1024)}, u32[]{:S(2)}) copy-start(f32[768]{0:T(1024)} %param.27) | copy-start | bytes 9220
  298.8 26.1 %all-gather.15.cloned.1.call-start = ((), (), s32[]{:S(2)}) async-start(), calls=%async_computation.13 | async-start | bytes 2359296 | tf_op jit(solution)/shard_map/all_gather | solution.py:150
  314.0 40.0 %reduce-scatter.12.cloned.1.call-start = ((), (), s32[]{:S(2)}) async-start(), calls=%async_computation.14 | async-start | bytes 4718592 | tf_op jit(solution)/shard_map/reduce_scatter | solution.py:158
  324.9 12.6 %copy-start.41 = (bf16[768,1536]{1,0:T(8,128)(2,1)S(1)}, bf16[768,1536]{1,0:T(8,128)(2,1)}, u32[]{:S(2)}) copy-start(bf16[768,1536]{1,0:T(8,128)(2,1)} %all-gather.11.cloned.1.call-done) | copy-start | bytes 7077892
  341.9 29.6 %all-gather.17.cloned.1.call-start = ((), (), s32[]{:S(2)}) async-start(), calls=%async_computation.15 | async-start | bytes 2359296 | tf_op jit(solution)/shard_map/all_gather | solution.py:165
  356.8 14.7 %copy-start.24 = (bf16[384,768]{0,1:T(8,128)(2,1)S(1)}, bf16[384,768]{0,1:T(8,128)(2,1)}, u32[]{:S(2)}) copy-start(bf16[384,768]{0,1:T(8,128)(2,1)} %all_gather.22) | copy-start | bytes 1769476
  360.3 13.5 %copy-start.22 = (bf16[384,1024]{1,0:T(8,128)(2,1)S(1)}, bf16[384,1024]{1,0:T(8,128)(2,1)}, u32[]{:S(2)}) copy-start(bf16[384,1024]{1,0:T(8,128)(2,1)} %copy-done.21) | copy-start | bytes 2359300
  360.3 232.9 %reduce-scatter.14.cloned.1.call-start = ((), (), s32[]{:S(2)}) async-start(), calls=%async_computation.16 | async-start | bytes 2359296 | tf_op jit(solution)/shard_map/reduce_scatter | solution.py:242
  406.5 17.3 %copy-start.5 = (bf16[384,1024]{1,0:T(8,128)(2,1)S(1)}, bf16[384,1024]{1,0:T(8,128)(2,1)}, u32[]{:S(2)}) copy-start(bf16[384,1024]{1,0:T(8,128)(2,1)} %copy-done.4) | copy-start | bytes 2359300
  425.8 16.7 %copy-start.12 = (bf16[6,64,512]{2,1,0:T(8,128)(2,1)}, bf16[6,64,512]{2,1,0:T(8,128)(2,1)S(1)}, u32[]{:S(2)}) copy-start(bf16[6,64,512]{2,1,0:T(8,128)(2,1)S(1)} %fusion.28) | copy-start | bytes 1179652
  436.6 6.0 copy-start.14
  442.5 208.7 %all-reduce.5.cloned.1.call-start = ((), (), s32[]{:S(2)}) async-start(), calls=%async_computation.20 | async-start | bytes 9437184
  442.6 2.3 copy-start.44
  450.8 210.3 %reduce-scatter.20.cloned.1.call-start = ((), (), s32[]{:S(2)}) async-start(), calls=%async_computation.19 | async-start | bytes 5013504 | tf_op jit(solution)/shard_map/reduce_scatter | solution.py:257
  458.7 344.3 %reduce-scatter.18.cloned.1.call-start = ((), (), s32[]{:S(2)}) async-start(), calls=%async_computation.18 | async-start | bytes 5013504 | tf_op jit(solution)/shard_map/reduce_scatter | solution.py:256
  466.4 4.8 copy-start.47
  466.4 6.0 copy-start.32
  466.4 6.0 copy-start.34
  466.4 6.0 copy-start.35
  466.4 49.9 %copy-start.38 = (f32[6,64]{1,0:T(8,128)S(1)}, f32[6,64]{1,0:T(8,128)}, u32[]{:S(2)}) copy-start(f32[6,64]{1,0:T(8,128)} %get-tuple-element.148) | copy-start | bytes 4612
  466.4 49.9 %copy-start.13 = (bf16[6,64,512]{2,1,0:T(8,128)(2,1)S(1)}, bf16[6,64,512]{2,1,0:T(8,128)(2,1)}, u32[]{:S(2)}) copy-start(bf16[6,64,512]{2,1,0:T(8,128)(2,1)} %copy-done.12) | copy-start | bytes 1179652
  466.4 49.9 %copy-start.15 = (bf16[6,64,512]{2,1,0:T(8,128)(2,1)S(1)}, bf16[6,64,512]{2,1,0:T(8,128)(2,1)}, u32[]{:S(2)}) copy-start(bf16[6,64,512]{2,1,0:T(8,128)(2,1)} %copy-done.14) | copy-start | bytes 1179652
  466.5 50.1 %copy-start.36 = (f32[1536]{0:T(1024)S(1)}, f32[1536]{0:T(1024)}, u32[]{:S(2)}) copy-start(f32[1536]{0:T(1024)} %get-tuple-element.125) | copy-start | bytes 18436
  466.5 126.7 %copy-start.3 = (f32[512,768]{1,0:T(8,128)S(1)}, f32[512,768]{1,0:T(8,128)}, u32[]{:S(2)}) copy-start(f32[512,768]{1,0:T(8,128)} %copy-done.2) | copy-start | bytes 4718596
  466.5 465.4 %reduce-scatter.16.cloned.1.call-start = ((), (), s32[]{:S(2)}) async-start(), calls=%async_computation.17 | async-start | bytes 1253376 | tf_op jit(solution)/shard_map/reduce_scatter | solution.py:255
  (14 other events, 20.5 us)
Sparse Core Ops, SparseCore 0:
  15.2 11.1 all-gather.6
  153.1 6.7 reduce-scatter.7
  298.9 9.1 reduce-scatter.9
  360.4 11.0 all-gather.16
  442.7 10.2 reduce-scatter.13
  459.3 201.6 reduce-scatter.19
  666.8 136.1 reduce-scatter.17
  809.0 122.7 reduce-scatter.15
Sparse Core Ops, SparseCore 1:
  156.6 58.3 all-gather.10
  217.1 7.9 all-gather.8
  228.2 63.7 all-gather.12
  314.0 10.8 all-gather.14
  342.0 11.9 reduce-scatter.11
  450.9 200.3 all-reduce.4
